TPU v7x, 128 devices: a whole 4x4x4 slice. The times are simulated.
128 devices in a mesh: azi: 32 (over z, y, core), ax: 4 (over x).
Axes of the slice: x: 4, y: 4, z: 4, core: 2. Of those that a mesh axis runs over, the one named last changes fastest.
Arguments:
- surface_data: bfloat16 [1024, 64, 2, 512], P('azi', 'ax'), may hold values from -6 to 6
- panel_pos: bfloat16 [3, 1024, 64], P(None, 'azi', 'ax'), may hold values from -0.3984375 to 0.3984375
- panel_normal: bfloat16 [3, 1024, 64], P(None, 'azi', 'ax'), may hold values from -3 to 3
- panel_area: bfloat16 [1024, 64], P('azi', 'ax'), may hold values from 0.099609375 to 1
- obs_pos: float32 [3, 98304], P(None, ('azi', 'ax')), may hold values from -0.4 to 0.4
- obs_angles: float32 [2, 768], P(None, ('azi', 'ax')), may hold values from -3.140625 to 3.140625
- send_list: int32 [128, 128], P(('azi', 'ax')), may hold values from -1 to 3, as said below
- entry_source: int32 [768, 32], P(('azi', 'ax')), may hold values from -1 to 127, as said below
- entry_offset: int32 [768, 32], P(('azi', 'ax')), may hold values from 16 to 252
Outputs:
- obs_pressure: float32 [98304, 256], P(('azi', 'ax'))
Inputs may be any that keep to these rules, and one draw needn't show every extreme that they name: `send_list`: entry (s, r) is set to a block of device s exactly where some observer block of device r lists s in entry_source, and is -1 elsewhere. `entry_source`: each row lists distinct devices, its live entries first and -1 after them; some row has all 32 entries live.
All inputs are finite; a program needn't handle non-finite values.
Results may differ from a plain program's by a relative error of at most 0.0033.
Values may be sent and summed in bfloat16 or wider, within the bound.
A program may use at most 256 MiB of HBM per device.

v0:
```python
import math

import jax
import jax.numpy as jnp
from jax import lax
from jax.sharding import PartitionSpec as P

BLOCK = 128
WIN = 256


FOUR_PI = 4.0 * math.pi


def with_halo(block, sides, width, periodic):
    for axis, dim in sides:
        count = lax.axis_size(axis)
        forward = [(i, i + 1) for i in range(count - 1)]
        if periodic:
            forward.append((count - 1, 0))
        backward = [(target, source) for source, target in forward]
        low = lax.ppermute(
            lax.slice_in_dim(block, block.shape[dim] - width, None, axis=dim), axis, forward
        )
        high = lax.ppermute(lax.slice_in_dim(block, 0, width, axis=dim), axis, backward)
        block = jnp.concatenate([low, block, high], axis=dim)
    return block


def lagrange_taps(fraction):
    return jnp.stack(
        [
            -(fraction - 1.0) * (fraction - 2.0) * (fraction - 3.0) / 6.0,
            fraction * (fraction - 2.0) * (fraction - 3.0) / 2.0,
            -fraction * (fraction - 1.0) * (fraction - 3.0) / 2.0,
            fraction * (fraction - 1.0) * (fraction - 2.0) / 6.0,
        ],
        0,
    )


def entry_term(signal, geometry, observer, angles, offset):
    sample_count = signal.shape[2] - 5
    widened = signal.astype(jnp.float32)
    slopes = (0.5 * (widened[:, :, 2:] - widened[:, :, :-2])).astype(jnp.bfloat16)
    levels_cut = signal[:, :, 1:-1]
    sources = jnp.stack([slopes[:, 1], levels_cut[:, 0], slopes[:, 0]], 0)
    shifted = jnp.stack(
        [sources[:, :, lag_index : lag_index + sample_count] for lag_index in range(4)], 1
    )
    columns = shifted.reshape(-1, sample_count)
    direction = jnp.stack(
        [
            jnp.cos(angles[0]) * jnp.cos(angles[1]),
            jnp.sin(angles[0]) * jnp.cos(angles[1]),
            jnp.sin(angles[1]),
        ]
    )
    geometry_f = geometry.astype(jnp.float32)
    toward_obs = jnp.sum(direction[:, None] * observer, 0)
    toward_pan = jnp.sum(direction[:, None] * geometry_f[0:3], 0)
    facing = jnp.sum(direction[:, None] * geometry_f[3:6], 0)
    fraction = 1.5 + toward_obs[:, None] - toward_pan[None, :]
    inverse = 16.0 / (offset.astype(jnp.float32) + fraction)
    amplitudes = jnp.stack(
        [
            geometry_f[6][None, :] * inverse,
            facing[None, :] * inverse,
            facing[None, :] * inverse * inverse,
        ],
        0,
    )
    tap_weights = lagrange_taps(fraction)
    weights = amplitudes[:, None] * tap_weights[None] / FOUR_PI
    matrix = (
        jnp.transpose(weights, (2, 0, 1, 3)).reshape(fraction.shape[0], -1).astype(jnp.bfloat16)
    )
    return jnp.dot(matrix, columns, preferred_element_type=jnp.float32)


def body(
    surface_data,
    panel_pos,
    panel_normal,
    panel_area,
    obs_pos,
    obs_angles,
    send_list,
    entry_source,
    entry_offset,
):
    padded = with_halo(surface_data, (("azi", 0),), 1, True)
    widened = padded.astype(jnp.float32)
    azimuth_pass = 0.25 * (widened[:-2] + 2.0 * widened[1:-1] + widened[2:])
    framed = with_halo(azimuth_pass, (("ax", 1),), 1, False)
    filtered = (0.25 * (framed[:, :-2] + 2.0 * framed[:, 1:-1] + framed[:, 2:])).astype(
        jnp.bfloat16
    )
    block_size = BLOCK
    window = WIN
    buffer_len = filtered.shape[3]
    blocks_here = filtered.shape[0] * filtered.shape[1] // block_size
    panel_blocks = filtered.reshape(blocks_here, block_size, 2, buffer_len)
    geometry = (
        jnp.concatenate([panel_pos, panel_normal, panel_area[None]], 0)
        .reshape(7, blocks_here, block_size)
        .transpose(1, 0, 2)
    )
    targets = send_list[0]
    devices = targets.shape[0]
    chosen = jnp.clip(targets, 0, blocks_here - 1)
    live_slot = targets >= 0
    outgoing = jnp.where(
        live_slot[:, None, None, None], panel_blocks[chosen], jnp.zeros((), jnp.bfloat16)
    )
    out_geometry = jnp.where(
        live_slot[:, None, None], geometry[chosen], jnp.zeros((), jnp.bfloat16)
    )
    arrived, arrived_geometry = (
        lax.all_to_all(outgoing, ("azi", "ax"), split_axis=0, concat_axis=0, tiled=True),
        lax.all_to_all(out_geometry, ("azi", "ax"), split_axis=0, concat_axis=0, tiled=True),
    )
    observer_blocks = obs_pos.reshape(3, -1, block_size).transpose(1, 0, 2)
    angle_rows = obs_angles.T

    def per_block(block_items):
        sources, offsets, observer, angles = block_items
        initial = jnp.zeros((block_size, window), jnp.float32)

        def add_entry(entry_index, running):
            source = sources[entry_index]
            offset = offsets[entry_index]
            slot_index = jnp.clip(source, 0, devices - 1)
            signal = lax.dynamic_slice(
                arrived, (slot_index, 0, 0, offset - 1), (1, block_size, 2, window + 5)
            )[0]
            geom_slot = lax.dynamic_index_in_dim(arrived_geometry, slot_index, 0, keepdims=False)
            contribution = entry_term(signal, geom_slot, observer, angles, offset)
            return running + jnp.where(source >= 0, contribution, 0.0)

        return lax.fori_loop(0, sources.shape[0], add_entry, initial)

    totals = lax.map(per_block, (entry_source, entry_offset, observer_blocks, angle_rows))
    return totals.reshape(-1, window)


def solution(mesh):
    in_specs = (
        P("azi", "ax", None, None),
        P(None, "azi", "ax"),
        P(None, "azi", "ax"),
        P("azi", "ax"),
        P(None, ("azi", "ax")),
        P(None, ("azi", "ax")),
        P(("azi", "ax"), None),
        P(("azi", "ax"), None),
        P(("azi", "ax"), None),
    )
    out_specs = P(("azi", "ax"), None)
    return jax.shard_map(body, mesh=mesh, in_specs=in_specs, out_specs=out_specs, check_vma=False)
```

profile of v0, /device:TPU:67, one launch (start us, length us, event | category | flops | bytes accessed | tf_op | source)
XLA Modules:
  0.0 1934.4 jit_solution(7587347430536115859)
XLA Ops:
  0.0 1.5 copy.31
  1.5 1.9 collective-permute-start
  5.5 1.6 collective-permute-done.1
  8.5 1.3 copy-done
  10.1 3.1 collective-permute-start.2
  13.2 2.2 collective-permute-start.3
  16.3 11.1 all-to-all-start
  27.4 3.4 fusion.37
  30.9 12.5 gather_fusion.1
  43.4 22.7 %broadcast_select_fusion = bf16[128,128,2,512]{3,1,2,0:T(8,128)(2,1)} fusion(bf16[128,128,2,512]{3,1,2,0:T(8,128)(2,1)} %gather_fusion.1, pred[128]{0:T(512)(128)(4,1)S(1)} %compare_bitcast_fusion), kind=kLoop, calls=%fused_computation.70 | loop fusion | flops 16777216 | bytes 67108992 | tf_op jit(solution)/shard_map/jit(_where)/select_n | solution.py:113
  66.1 10.2 all-to-all-start.1
  76.4 542.4 %all-to-all-done.1 = bf16[128,128,2,512]{3,1,2,0:T(8,128)(2,1)} async-done(((bf16[128,128,2,512]{3,1,2,0:T(8,128)(2,1)}), bf16[128,128,2,512]{3,1,2,0:T(8,128)(2,1)}, u32[]{:S(2)}, u32[]{:S(2)}) %all-to-all-start.1) | async-done | bytes 33554464 | tf_op jit(solution)/shard_map/all_to_all | solution.py:120
  618.8 1314.7 %while.45 = (s32[]{:T(128)}, f32[6,128,256]{2,1,0:T(8,128)S(1)}, s32[6,32]{1,0:T(8,128)}, s32[6,32]{1,0:T(8,128)}, f32[6,3,128]{2,1,0:T(4,128)}, /*index=5*/f32[...) while((s32[]{:T(128)}, f32[6,128,256]{2,1,0:T(8,128)S(1)}, ...), condition=%wide.region_6.7_spmd, body=%wide.region_0.6_spmd.sunk | while | flops 103670416 | bytes 6731688 | solution.py:143
  623.7 214.2 %while.46 = (s32[]{:T(128)}, f32[128,256]{1,0:T(8,128)S(1)}, s32[32]{0:T(128)S(1)}, bf16[128,7,128]{2,1,0:T(8,128)(2,1)S(1)}, s32[32]{0:T(128)S(1)}, /*index=5*/...) while((s32[]{:T(128)}, f32[128,256]{1,0:T(8,128)S(1)}, ...), condition=%wide.region_5.5_spmd.clone, body=%wide.region_1.4_spmd.clone.sunk | while | flops 103670408 | bytes 6465563 | solution.py:141
  627.7 1.1 fusion.56
  634.4 1.1 fusion.56
  674.5 1.1 fusion.56
  681.2 1.1 fusion.56
  687.9 1.1 fusion.56
  694.6 1.1 fusion.56
  701.3 1.1 fusion.56
  708.0 1.1 fusion.56
  714.7 1.1 fusion.56
  728.1 1.1 fusion.56
  748.2 1.1 fusion.56
  754.9 1.1 fusion.56
  761.6 1.1 fusion.56
  775.0 1.1 fusion.56
  781.7 1.1 fusion.56
  788.4 1.1 fusion.56
  801.7 1.1 fusion.56
  808.4 1.1 fusion.56
  842.9 214.0 %while.46 = (s32[]{:T(128)}, f32[128,256]{1,0:T(8,128)S(1)}, s32[32]{0:T(128)S(1)}, bf16[128,7,128]{2,1,0:T(8,128)(2,1)S(1)}, s32[32]{0:T(128)S(1)}, /*index=5*/...) while((s32[]{:T(128)}, f32[128,256]{1,0:T(8,128)S(1)}, ...), condition=%wide.region_5.5_spmd.clone, body=%wide.region_1.4_spmd.clone.sunk | while | flops 103670408 | bytes 6465563 | solution.py:141
  860.2 1.1 fusion.56
  873.6 1.1 fusion.56
  900.4 1.1 fusion.56
  933.8 1.1 fusion.56
  953.8 1.1 fusion.56
  987.3 1.1 fusion.56
  1027.4 1.1 fusion.56
  1040.8 1.1 fusion.56
  1047.5 1.1 fusion.56
  1061.9 214.1 %while.46 = (s32[]{:T(128)}, f32[128,256]{1,0:T(8,128)S(1)}, s32[32]{0:T(128)S(1)}, bf16[128,7,128]{2,1,0:T(8,128)(2,1)S(1)}, s32[32]{0:T(128)S(1)}, /*index=5*/...) while((s32[]{:T(128)}, f32[128,256]{1,0:T(8,128)S(1)}, ...), condition=%wide.region_5.5_spmd.clone, body=%wide.region_1.4_spmd.clone.sunk | while | flops 103670408 | bytes 6465563 | solution.py:141
  1065.8 1.1 fusion.56
  1079.2 1.1 fusion.56
  1281.0 214.2 %while.46 = (s32[]{:T(128)}, f32[128,256]{1,0:T(8,128)S(1)}, s32[32]{0:T(128)S(1)}, bf16[128,7,128]{2,1,0:T(8,128)(2,1)S(1)}, s32[32]{0:T(128)S(1)}, /*index=5*/...) while((s32[]{:T(128)}, f32[128,256]{1,0:T(8,128)S(1)}, ...), condition=%wide.region_5.5_spmd.clone, body=%wide.region_1.4_spmd.clone.sunk | while | flops 103670408 | bytes 6465563 | solution.py:141
  1500.2 214.1 %while.46 = (s32[]{:T(128)}, f32[128,256]{1,0:T(8,128)S(1)}, s32[32]{0:T(128)S(1)}, bf16[128,7,128]{2,1,0:T(8,128)(2,1)S(1)}, s32[32]{0:T(128)S(1)}, /*index=5*/...) while((s32[]{:T(128)}, f32[128,256]{1,0:T(8,128)S(1)}, ...), condition=%wide.region_5.5_spmd.clone, body=%wide.region_1.4_spmd.clone.sunk | while | flops 103670408 | bytes 6465563 | solution.py:141
  1719.4 214.0 %while.46 = (s32[]{:T(128)}, f32[128,256]{1,0:T(8,128)S(1)}, s32[32]{0:T(128)S(1)}, bf16[128,7,128]{2,1,0:T(8,128)(2,1)S(1)}, s32[32]{0:T(128)S(1)}, /*index=5*/...) while((s32[]{:T(128)}, f32[128,256]{1,0:T(8,128)S(1)}, ...), condition=%wide.region_5.5_spmd.clone, body=%wide.region_1.4_spmd.clone.sunk | while | flops 103670408 | bytes 6465563 | solution.py:141
  (2933 shorter events, 657.8 us)
Async XLA Ops:
  0.0 3.5 copy-start.7
  0.0 3.5 copy-start.3
  0.0 3.7 copy-start.4
  0.0 3.9 copy-start.5
  1.5 3.3 collective-permute-start
  3.5 3.6 collective-permute-start.1
  4.8 0.6 copy-start.1
  8.5 1.3 copy-start
  10.1 17.3 collective-permute-start.2
  13.2 14.2 collective-permute-start.3
  16.3 49.8 %all-to-all-start = ((bf16[128,7,128]{2,1,0:T(8,128)(2,1)}), bf16[128,7,128]{2,1,0:T(8,128)(2,1)S(1)}, u32[]{:S(2)}, u32[]{:S(2)}) async-start(bf16[128,7,128]{2,1,0:T(8,128)(2,1)} %broadcast_select_fusion.1), calls=%async_computation | async-start | bytes 524288 | tf_op jit(solution)/shard_map/all_to_all | solution.py:121
  66.1 552.6 %copy-start.2 = (f32[2,6]{1,0:T(2,128)S(1)}, f32[2,6]{1,0:T(2,128)}, u32[]{:S(2)}) copy-start(f32[2,6]{1,0:T(2,128)} %param.18) | copy-start | bytes 148
  66.1 552.6 %all-to-all-start.1 = ((bf16[128,128,2,512]{3,1,2,0:T(8,128)(2,1)}), bf16[128,128,2,512]{3,1,2,0:T(8,128)(2,1)}, u32[]{:S(2)}, u32[]{:S(2)}) async-start(bf16[128,128,2,512]{3,1,2,0:T(8,128)(2,1)} %broadcast_select_fusion), calls=%async_computation.1 | async-start | bytes 67108864 | tf_op jit(solution)/shard_map/all_to_all | solution.py:120
  1933.5 0.9 copy-start.6
where the time goes:
time: 1950 us; the launch traced here: 1930 us
  loops' own time  631 us (32%)
  waiting for transfers between devices  544 us (28%)
  local copies, waits for them, and re-layouts  336 us (17%)
  other arithmetic  329 us (17%)
  matrix products  65.5 us (3%)
  starting transfers between devices  28.5 us (1%)
    another operation x6, loops' own time, per_block(): return lax.fori_loop(0, sources.shape[0], add_entry, initial)  614 us
    all_to_all x1, waiting for transfers between devices, body(): lax.all_to_all(outgoing, ('azi', 'ax'), split_axis=0, concat_axis=0, tile...  542 us
    convert_element_type x192, other arithmetic, entry_term(): widened = signal.astype(jnp.float32)  205 us
    dynamic_slice x192, local copies, waits for them, and re-layouts, add_entry(): source = sources[entry_index]  127 us
    dynamic_slice x192, local copies, waits for them, and re-layouts, add_entry(): offset = offsets[entry_index]  114 us
    dot_general x192, matrix products, entry_term(): return jnp.dot(matrix, columns, preferred_element_type=jnp.float32)  65.5 us
    another operation x192, local copies, waits for them, and re-layouts, entry_term(): jnp.stack([sources[:, :, lag_index:lag_index + sample_count] for lag_inde...  43.9 us
  transfers between devices with their start and end apart: 6, of which 2 were waited for; matrix products, arithmetic and copies ran while one was open for 2% of the time, Pallas kernels for 0%

commit v1 on v0

v1 whole, which is shorter than its diff:
```python
import math

import jax
import jax.numpy as jnp
from jax import lax
from jax.experimental import pallas as pl
from jax.experimental.pallas import tpu as pltpu
from jax.sharding import Mesh
from jax.sharding import PartitionSpec as P

BLOCK = 128
WIN = 256
BUF = 512
BLOCKS_HERE = 4
OWN = 6
NZ, NY, NC, NX = 4, 4, 2, 4
LINES = NZ * NY
GROUP = NC * NX
SLOTS = GROUP * BLOCKS_HERE
ROWS = LINES * OWN
SPAN = 272
PADDED = 528
FOUR_PI = 4.0 * math.pi
AZI = ("z", "y", "core")


def filter_local(surface_data):
    count = lax.axis_size("ax")
    up = [(i, i + 1) for i in range(count - 1)]
    down = [(b, a) for a, b in up]
    low = lax.ppermute(surface_data[:, -1:], "ax", up)
    high = lax.ppermute(surface_data[:, :1], "ax", down)
    framed = jnp.concatenate([low, surface_data, high], axis=1)
    count = NZ * NY * NC
    ring = [(i, (i + 1) % count) for i in range(count)]
    back = [(b, a) for a, b in ring]
    low = lax.ppermute(framed[-1:], AZI, ring)
    high = lax.ppermute(framed[:1], AZI, back)
    widened = jnp.concatenate([low, framed, high], axis=0).astype(jnp.float32)
    passed = 0.25 * (widened[:-2] + 2.0 * widened[1:-1] + widened[2:])
    filtered = 0.25 * (passed[:, :-2] + 2.0 * passed[:, 1:-1] + passed[:, 2:])
    return filtered.astype(jnp.bfloat16)


def entry_codes(sources, offsets, table, line):
    units = jnp.arange(GROUP, dtype=jnp.int32)
    wanted = line * GROUP + units
    match = sources[:, None, :] == wanted[None, :, None]
    offset = jnp.max(jnp.where(match, offsets[:, None, :], -1), axis=2)
    block = jnp.repeat(table.T, OWN, axis=0)
    live = (offset >= 0) & (block >= 0)
    code = offset * SLOTS + units[None, :] * BLOCKS_HERE + block
    place = jnp.cumsum(live.astype(jnp.int32), axis=1) - 1
    hit = live[:, :, None] & (place[:, :, None] == units[None, None, :])
    packed = jnp.sum(jnp.where(hit, code[:, :, None], 0), axis=1)
    return packed, jnp.sum(live.astype(jnp.int32), axis=1)


def partial_kernel(codes, counts, dirs, toward, geometry, signals, out, source, weights, total, reach_obs):
    def build(slot, carry):
        level = signals[slot].astype(jnp.float32)
        slope = 0.5 * (pltpu.roll(level, BUF - 1, 0) - pltpu.roll(level, 1, 0))
        slope = slope.astype(jnp.bfloat16).astype(jnp.float32)
        source[slot * 3, 0:BUF, :] = slope[:, 128:256]
        source[slot * 3 + 1, 0:BUF, :] = level[:, 0:128]
        source[slot * 3 + 2, 0:BUF, :] = slope[:, 0:128]
        for kind in range(3):
            source[slot * 3 + kind, BUF:PADDED, :] = jnp.zeros((PADDED - BUF, 128), jnp.float32)
        return carry

    lax.fori_loop(0, SLOTS, build, 0)

    def per_row(row, carry):
        d0, d1, d2 = dirs[row * 3], dirs[row * 3 + 1], dirs[row * 3 + 2]
        total[...] = jnp.zeros_like(total)
        line = jnp.broadcast_to(toward[pl.ds(row, 1), :], (BLOCK, BLOCK))
        reach_obs[...] = 1.5 + line.T

        def per_entry(position, inner):
            code = codes[row * GROUP + position]
            slot = lax.rem(code, SLOTS)
            offset = lax.div(code, SLOTS)
            offset_f = offset.astype(jnp.float32)
            geo = geometry[slot]
            toward_pan = d0 * geo[0:1] + d1 * geo[1:2] + d2 * geo[2:3]
            facing = (d0 * geo[3:4] + d1 * geo[4:5] + d2 * geo[5:6]) * (1.0 / FOUR_PI)
            area = geo[6:7] * (1.0 / FOUR_PI)
            for chunk in range(BLOCK // 16):
                fraction = reach_obs[chunk * 16 : chunk * 16 + 16, :] - toward_pan
                inverse = 16.0 / (offset_f + fraction)
                strength = facing * inverse
                amplitudes = (area * inverse, strength, strength * inverse)
                f1, f2, f3 = fraction - 1.0, fraction - 2.0, fraction - 3.0
                front, rear = fraction * f1, f2 * f3
                taps = (
                    f1 * rear * (-1.0 / 6.0),
                    fraction * rear * 0.5,
                    front * f3 * -0.5,
                    front * f2 * (1.0 / 6.0),
                )
                for tap_index in range(4):
                    pair, parity = divmod(tap_index, 2)
                    for kind in range(3):
                        column = (pair * 3 + kind) * 128
                        weights[
                            parity * 128 + chunk * 16 : parity * 128 + chunk * 16 + 16, column : column + 128
                        ] = (amplitudes[kind] * taps[tap_index]).astype(jnp.bfloat16)
            columns = jnp.concatenate(
                [
                    source[slot * 3 + kind, pl.ds(offset + 2 * pair, SPAN), :].astype(jnp.bfloat16)
                    for pair in range(2)
                    for kind in range(3)
                ],
                axis=1,
            )
            total[...] += lax.dot_general(
                columns, weights[...], (((1,), (1,)), ((), ())), preferred_element_type=jnp.float32
            )
            return inner

        lax.fori_loop(0, counts[row], per_entry, 0)
        out[row] = (total[0:WIN, 0:128] + total[1 : WIN + 1, 128:256]).astype(jnp.bfloat16)
        return carry

    lax.fori_loop(0, ROWS, per_row, 0)


def partial_sums(codes, counts, dirs, toward, geometry, signals, interpret=False):
    smem = pl.BlockSpec(memory_space=pltpu.SMEM)
    vmem = pl.BlockSpec(memory_space=pltpu.VMEM)
    return pl.pallas_call(
        partial_kernel,
        out_shape=jax.ShapeDtypeStruct((ROWS, WIN, BLOCK), jnp.bfloat16),
        in_specs=[smem, smem, smem, vmem, vmem, vmem],
        out_specs=vmem,
        scratch_shapes=[
            pltpu.VMEM((SLOTS * 3, PADDED, 128), jnp.float32),
            pltpu.VMEM((256, 768), jnp.bfloat16),
            pltpu.VMEM((SPAN, 256), jnp.float32),
            pltpu.VMEM((BLOCK, BLOCK), jnp.float32),
        ],
        compiler_params=pltpu.CompilerParams(vmem_limit_bytes=60 * 1024 * 1024),
        interpret=interpret,
    )(codes, counts, dirs, toward, geometry, signals)


def directions(angles):
    u, v = angles[..., 0], angles[..., 1]
    return jnp.stack([jnp.cos(u) * jnp.cos(v), jnp.sin(u) * jnp.cos(v), jnp.sin(v)], -1)


def body(
    surface_data,
    panel_pos,
    panel_normal,
    panel_area,
    obs_pos,
    obs_angles,
    send_list,
    entry_source,
    entry_offset,
):
    z, y = lax.axis_index("z"), lax.axis_index("y")
    core, ax = lax.axis_index("core"), lax.axis_index("ax")
    line = z * NY + y

    asked = jnp.concatenate(
        [
            obs_pos.reshape(-1),
            obs_angles.T.reshape(-1),
            entry_source.astype(jnp.float32).reshape(-1),
            entry_offset.astype(jnp.float32).reshape(-1),
        ]
    )
    asked = lax.all_gather(asked, ("z", "y"))
    n_pos, n_ang, n_ent = 3 * OWN * BLOCK, 2 * OWN, OWN * 32
    pos = asked[:, :n_pos].reshape(LINES, 3, OWN, BLOCK).transpose(0, 2, 1, 3).reshape(ROWS, 3, BLOCK)
    dirs = directions(asked[:, n_pos : n_pos + n_ang].reshape(ROWS, 2))
    entries = asked[:, n_pos + n_ang :].astype(jnp.int32)
    sources = entries[:, :n_ent].reshape(ROWS, 32)
    offsets = entries[:, n_ent:].reshape(ROWS, 32)
    toward = jnp.sum(dirs[:, :, None] * pos, axis=1)

    filtered = filter_local(surface_data)
    panels = filtered.reshape(BLOCKS_HERE, BLOCK, 2, BUF).transpose(0, 3, 2, 1).reshape(-1, 2 * BLOCK)
    geometry = jnp.concatenate(
        [panel_pos, panel_normal, panel_area[None], jnp.zeros_like(panel_area)[None]], 0
    ).reshape(8, BLOCKS_HERE, BLOCK).transpose(1, 0, 2)
    listed = send_list.astype(jnp.bfloat16)
    small = jnp.concatenate([geometry.reshape(-1), listed.reshape(-1), jnp.zeros((128,), jnp.bfloat16)])
    small_rows = small.shape[0] // 256
    small = jnp.pad(small.reshape(small_rows, 256), ((0, 32 - small_rows), (0, 0)))
    gathered = lax.all_gather(jnp.concatenate([panels, small], 0), ("core", "ax"))
    signals = gathered[:, : BLOCKS_HERE * BUF].reshape(SLOTS, BUF, 2 * BLOCK)
    small = gathered[:, BLOCKS_HERE * BUF :].reshape(GROUP, -1)
    geometry = small[:, : BLOCKS_HERE * 8 * BLOCK].reshape(SLOTS, 8, BLOCK).astype(jnp.float32)
    listed = small[:, BLOCKS_HERE * 8 * BLOCK : BLOCKS_HERE * 8 * BLOCK + 128].astype(jnp.int32)
    table = listed.reshape(GROUP, LINES, NC, NX)
    table = lax.dynamic_slice(table, (0, 0, core, ax), (GROUP, LINES, 1, 1)).reshape(GROUP, LINES)

    packed, counts = entry_codes(sources, offsets, table, line)
    sums = partial_sums(packed.reshape(-1), counts, dirs.reshape(-1), toward, geometry, signals)

    sums = sums.reshape(NZ, NY, OWN, WIN, BLOCK)
    sums = lax.all_to_all(sums, "y", split_axis=1, concat_axis=1, tiled=True)
    sums = jnp.sum(sums.astype(jnp.float32), axis=1).astype(jnp.bfloat16)
    sums = lax.all_to_all(sums, "z", split_axis=0, concat_axis=0, tiled=True)
    sums = jnp.sum(sums.astype(jnp.float32), axis=0)
    return sums.transpose(0, 2, 1).reshape(OWN * BLOCK, WIN)


def solution(mesh):
    split = Mesh(mesh.devices.reshape(NZ, NY, NC, NX), ("z", "y", "core", "ax"))
    azi, every = AZI, AZI + ("ax",)
    in_specs = (
        P(azi, "ax", None, None),
        P(None, azi, "ax"),
        P(None, azi, "ax"),
        P(azi, "ax"),
        P(None, every),
        P(None, every),
        P(every, None),
        P(every, None),
        P(every, None),
    )
    return jax.shard_map(body, mesh=split, in_specs=in_specs, out_specs=P(every, None), check_vma=False)
```

time: 1950 us -> 287 us (0.15)
  the two profiles are of different devices: /device:TPU:67 before, /device:TPU:0 now
where the time goes in v1:
time: 287 us; the launch traced here: 286 us
  blocking collectives  102 us (36%)
  waiting for transfers between devices  65.1 us (23%)
  Pallas kernels  46.1 us (16%)
  local copies, waits for them, and re-layouts  30.1 us (10%)
  other arithmetic  15.9 us (6%)
  between operations  15.8 us (6%)
  starting transfers between devices  10.6 us (4%)
    all_to_all x1, blocking collectives, body(): sums = lax.all_to_all(sums, 'y', split_axis=1, concat_axis=1, tiled=True)  74.2 us
    unnamed x3, waiting for transfers between devices  63.5 us
    pallas_call x1, Pallas kernels, partial_sums(): pl.pallas_call(partial_kernel, out_shape=jax.ShapeDtypeStruct((ROWS, WIN,...  46.1 us
    all_to_all x1, blocking collectives, body(): sums = lax.all_to_all(sums, 'z', split_axis=0, concat_axis=0, tiled=True)  28.1 us
    unnamed x15, local copies, waits for them, and re-layouts  8.51 us
    slice x1, local copies, waits for them, and re-layouts, body(): signals = gathered[:, :BLOCKS_HERE * BUF].reshape(SLOTS, BUF, 2 * BLOCK)  7.15 us
  transfers between devices with their start and end apart: 6, of which 3 were waited for; matrix products, arithmetic and copies ran while one was open for 9% of the time, Pallas kernels for 0%

profile of v1, /device:TPU:0, one launch (start us, length us, event | category | flops | bytes accessed | tf_op | source)
XLA Modules:
  0.0 285.9 jit_solution(5539721317137472551)
XLA Ops:
  7.4 1.0 fusion.11
  8.3 3.5 %collective-permute-start = (bf16[32,1,2,512]{3,2,1,0:T(2,128)(2,1)S(1)}, bf16[32,1,2,512]{3,2,1,0:T(2,128)(2,1)S(1)}, u32[]{:S(2)}, u32[]{:S(2)}) collective-permute-start(bf16[32,1,2,512]{3,2,1,0:T(2,128)(2,1)S(1)} %get-tuple-element.12), channel_id=1, source_target_pairs={{0,1},{1,2},{2,3},{4,5},{5,6},{6,7},{8,9},{9,10},{10,11},{12,13},{... | collective-permute-start | bytes 196616 | tf_op jit(solution)/shard_map/ppermute | solution.py:31
  11.8 1.3 collective-permute-start.1
  13.1 0.7 reshape.144
  13.9 0.7 convert_element_type.45
  14.6 0.7 convert_element_type.46
  15.4 0.8 copy.77
  16.2 1.2 dynamic-slice
  18.2 0.3 dynamic-update-slice
  18.6 0.7 copy-done
  19.3 0.8 copy.81
  20.1 0.1 concatenate.28
  20.2 0.8 copy.82
  21.0 0.1 concatenate.29
  21.1 0.8 copy.83
  22.1 0.7 convert_bitcast_fusion
  22.9 2.6 constant_dynamic-update-slice_fusion.1
  25.6 5.7 %collective-permute-start.3 = (bf16[1,18,2,512]{3,2,1,0:T(2,128)(2,1)S(1)}, bf16[1,18,2,512]{3,2,1,0:T(2,128)(2,1)S(1)}, u32[]{:S(2)}, u32[]{:S(2)}) collective-permute-start(bf16[1,18,2,512]{3,2,1,0:T(2,128)(2,1)S(1)} %get-tuple-element.10), channel_id=1, source_target_pairs={{4,0},{8,4},{12,8},{16,12},{20,16},{24,20},{28,24},{32,28},{36,32}... | collective-permute-start | bytes 110600 | tf_op jit(solution)/shard_map/ppermute | solution.py:38
  31.4 1.5 collective-permute-done.2
  33.0 1.6 maximum_convert_fusion
  34.6 3.3 %fusion = f32[32,18,2,512]{3,2,1,0:T(2,128)S(1)} fusion(f32[34,18,2,512]{3,2,1,0:T(2,128)S(1)} %maximum_convert_fusion), kind=kLoop, calls=%fused_computation.2 | loop fusion | flops 2359296 | bytes 9437184 | tf_op jit(solution)/shard_map/mul | solution.py:40
  37.9 2.3 fusion.4
  40.2 1.5 copy.80
  41.7 0.1 copy.100
  41.9 1.1 fusion.6
  43.1 63.5 %all-reduce.4.cloned.1.call-done = f32[43200]{0:T(1024)} async-done(((f32[43200]{0:T(1024)}), f32[43200]{0:T(1024)}) %all-reduce.4.cloned.1.call-update) | async-done | bytes 172816
  106.5 1.1 reshape.168
  108.2 0.1 copy.90
  108.8 0.1 fusion.7
  108.9 0.6 reduce_sum.53.toward
  109.5 0.8 reshape.160.dirs
  110.3 0.1 select_reduce_fusion
  110.4 0.9 slice_bitcast_fusion
  111.5 7.1 %slice.102 = bf16[8,2048,256]{2,1,0:T(8,128)(2,1)} slice(bf16[8,2080,256]{2,1,0:T(8,128)(2,1)} %bitcast.43), slice={[0:8], [0:2048], [0:256]} | slice | bytes 16777216 | tf_op jit(solution)/shard_map/slice | solution.py:194
  118.6 0.1 copy.85
  118.9 0.1 reshape.157
  119.1 0.1 broadcast_in_dim.52
  119.2 0.6 convert_reduce_fusion.1
  119.8 0.1 copy.87
  119.9 0.7 reshape.158.codes
  120.6 0.7 reshape.167.geometry
  121.3 46.1 %shard_map.91 = bf16[96,256,128]{2,1,0:T(8,128)(2,1)} custom-call(s32[768]{0:T(1024)} %reshape.158.codes, s32[96]{0:T(128)} %get-tuple-element.5.counts, f32[288]{0:T(512)} %reshape.160.dirs, f32[96,128]{1,0:T(8,128)} %reduce_sum.53.toward, f32[32,8,128]{2,1,0:T(8,128)} %reshape.167.geometry, bf16[32,512,256]{2,1,0:T(8,128)(2,1)} %bitcast.40), custom_call_target="tpu_custom_call" | custom-call | tf_op jit(solution)/shard_map/pallas_call | solution.py:131
  167.4 3.2 %copy.92 = bf16[4,4,6,256,128]{4,3,2,0,1:T(8,128)(2,1)S(1)} copy(bf16[4,4,6,256,128]{4,3,2,1,0:T(8,128)(2,1)} %bitcast.41) | data formatting | bytes 12582912 | tf_op jit(solution)/shard_map/reshape | solution.py:204
  170.6 74.2 %all_to_all.10 = bf16[4,4,6,256,128]{4,3,2,0,1:T(8,128)(2,1)} all-to-all(bf16[4,4,6,256,128]{4,3,2,0,1:T(8,128)(2,1)S(1)} %copy.92), channel_id=1, replica_groups=mesh['z'=4,'y'=4,'core'=2,'ax'=4] {'y'}, dimensions={1} | all-to-all | bytes 12582912 | tf_op jit(solution)/shard_map/all_to_all | solution.py:205
  244.8 4.1 %reduce_sum.54 = bf16[4,6,256,128]{3,2,1,0:T(8,128)(2,1)S(1)} reduce(bf16[4,4,6,256,128]{4,3,2,0,1:T(8,128)(2,1)} %all_to_all.10, bf16[]{:T(256)} %constant.13.clone.1), dimensions={1}, to_apply=%region_5.6 | reduce | flops 2359296 | bytes 7864322 | tf_op jit(solution)/shard_map/reduce_sum | solution.py:206
  249.0 28.1 %all_to_all.11 = bf16[4,6,256,128]{3,2,1,0:T(8,128)(2,1)S(1)} all-to-all(bf16[4,6,256,128]{3,2,1,0:T(8,128)(2,1)S(1)} %reduce_sum.54), channel_id=1, replica_groups=mesh['z'=4,'y'=4,'core'=2,'ax'=4] {'z'}, dimensions={0} | all-to-all | bytes 3145728 | tf_op jit(solution)/shard_map/all_to_all | solution.py:207
  277.1 0.2 convert_reduce_fusion
  277.3 1.1 copy.93
  (57 shorter events, 2.4 us)
Async XLA Ops:
  7.4 99.2 %all-reduce.4.cloned.1.call-start = ((), (), s32[]{:S(2)}) async-start(), calls=%async_computation.3 | async-start | bytes 352256
  8.3 14.5 %collective-permute-start = (bf16[32,1,2,512]{3,2,1,0:T(2,128)(2,1)S(1)}, bf16[32,1,2,512]{3,2,1,0:T(2,128)(2,1)S(1)}, u32[]{:S(2)}, u32[]{:S(2)}) collective-permute-start(bf16[32,1,2,512]{3,2,1,0:T(2,128)(2,1)S(1)} %get-tuple-element.12), channel_id=1, source_target_pairs={{0,1},{1,2},{2,3},{4,5},{5,6},{6,7},{8,9},{9,10},{10,11},{12,13},{... | collective-permute-start | bytes 196616 | tf_op jit(solution)/shard_map/ppermute | solution.py:31
  11.8 13.6 %collective-permute-start.1 = (bf16[32,1,2,512]{3,2,1,0:T(2,128)(2,1)S(1)}, bf16[32,1,2,512]{3,2,1,0:T(2,128)(2,1)S(1)}, u32[]{:S(2)}, u32[]{:S(2)}) collective-permute-start(bf16[32,1,2,512]{3,2,1,0:T(2,128)(2,1)S(1)} %get-tuple-element.11), channel_id=1, source_target_pairs={{1,0},{2,1},{3,2},{5,4},{6,5},{7,6},{9,8},{10,9},{11,10},{13,12},{... | collective-permute-start | bytes 196616 | tf_op jit(solution)/shard_map/ppermute | solution.py:32
  18.6 0.7 copy-start
  19.3 91.2 %all-gather.4.cloned.1.call-start = ((), (), s32[]{:S(2)}) async-start(), calls=%async_computation.2 | async-start | bytes 9584640 | tf_op jit(solution)/shard_map/all_gather | solution.py:193
  25.6 7.3 %collective-permute-start.2 = (bf16[1,18,2,512]{3,2,1,0:T(2,128)(2,1)S(1)}, bf16[1,18,2,512]{3,2,1,0:T(2,128)(2,1)S(1)}, u32[]{:S(2)}, u32[]{:S(2)}) collective-permute-start(bf16[1,18,2,512]{3,2,1,0:T(2,128)(2,1)S(1)} %get-tuple-element.9), channel_id=1, source_target_pairs={{0,4},{4,8},{8,12},{12,16},{16,20},{20,24},{24,28},{28,32},{32,36}... | collective-permute-start | bytes 110600 | tf_op jit(solution)/shard_map/ppermute | solution.py:37
  25.6 7.3 %collective-permute-start.3 = (bf16[1,18,2,512]{3,2,1,0:T(2,128)(2,1)S(1)}, bf16[1,18,2,512]{3,2,1,0:T(2,128)(2,1)S(1)}, u32[]{:S(2)}, u32[]{:S(2)}) collective-permute-start(bf16[1,18,2,512]{3,2,1,0:T(2,128)(2,1)S(1)} %get-tuple-element.10), channel_id=1, source_target_pairs={{4,0},{8,4},{12,8},{16,12},{20,16},{24,20},{28,24},{32,28},{36,32}... | collective-permute-start | bytes 110600 | tf_op jit(solution)/shard_map/ppermute | solution.py:38
Sparse Core Ops, SparseCore 0:
  19.4 87.1 all-reduce.3
Sparse Core Ops, SparseCore 1:
  43.1 52.4 all-gather.3

commit v2 on v1

--- a/solution.py
+++ b/solution.py
@@ -22,6 +22,7 @@
 PADDED = 528
 FOUR_PI = 4.0 * math.pi
 AZI = ("z", "y", "core")
+MESH = pl.DeviceIdType.MESH
 
 
 def filter_local(surface_data):
@@ -119,7 +120,8 @@
             return inner
 
         lax.fori_loop(0, counts[row], per_entry, 0)
-        out[row] = (total[0:WIN, 0:128] + total[1 : WIN + 1, 128:256]).astype(jnp.bfloat16)
+        out[0, row] = (total[0:128, 0:128] + total[1:129, 128:256]).astype(jnp.bfloat16)
+        out[1, row] = (total[128:256, 0:128] + total[129:257, 128:256]).astype(jnp.bfloat16)
         return carry
 
     lax.fori_loop(0, ROWS, per_row, 0)
@@ -130,7 +132,7 @@
     vmem = pl.BlockSpec(memory_space=pltpu.VMEM)
     return pl.pallas_call(
         partial_kernel,
-        out_shape=jax.ShapeDtypeStruct((ROWS, WIN, BLOCK), jnp.bfloat16),
+        out_shape=jax.ShapeDtypeStruct((2, ROWS, WIN // 2, BLOCK), jnp.bfloat16),
         in_specs=[smem, smem, smem, vmem, vmem, vmem],
         out_specs=vmem,
         scratch_shapes=[
@@ -142,6 +144,151 @@
         compiler_params=pltpu.CompilerParams(vmem_limit_bytes=60 * 1024 * 1024),
         interpret=interpret,
     )(codes, counts, dirs, toward, geometry, signals)
+
+
+def wrap(index):
+    return lax.rem(index + 4, 4)
+
+
+def reduce_kernel(sums, out, relay, message, forward, reduced, relay2, message2, forward2, send, recv):
+    z, y = lax.axis_index("z"), lax.axis_index("y")
+    axes = (("y", "z"), ("z", "y"))
+    places = ((y, z), (z, y))
+    barrier = pltpu.get_barrier_semaphore()
+    for axis, place in (("y", y), ("z", z)):
+        for step in (1, -1):
+            pl.semaphore_signal(barrier, inc=1, device_id={axis: wrap(place + step)}, device_id_type=MESH)
+    pl.semaphore_wait(barrier, 4)
+
+    def piece(half, first, second):
+        if half == 0:
+            return sums.at[0, second, first]
+        return sums.at[1, first, second]
+
+    def copy(number, half, stage, step, src, dst):
+        axis = axes[half][stage]
+        return pltpu.make_async_remote_copy(
+            src_ref=src,
+            dst_ref=dst,
+            send_sem=send.at[half, stage, number],
+            recv_sem=recv.at[half, stage, number],
+            device_id={axis: wrap(places[half][stage] + step)},
+            device_id_type=MESH,
+        )
+
+    low, high = pl.ds(0, 2), pl.ds(2, 2)
+    first_copies = []
+    for half in range(2):
+        me = places[half][0]
+        there, after, before = wrap(me + 2), wrap(me + 1), wrap(me - 1)
+        batch = [
+            copy(0, half, 0, 1, piece(half, there, low), relay.at[half, 0]),
+            copy(1, half, 0, -1, piece(half, there, high), relay.at[half, 1]),
+            copy(2, half, 0, 1, piece(half, after, high), message.at[half, 0, high]),
+            copy(3, half, 0, -1, piece(half, before, low), message.at[half, 1, low]),
+        ]
+        first_copies.append(batch)
+    for number in range(4):
+        for half in range(2):
+            first_copies[half][number].start()
+
+    for half in range(2):
+        me = places[half][0]
+        for side, step, offset in ((0, 1, 0), (1, -1, 2)):
+            first_copies[half][side].wait_recv()
+
+            def add_relay(index, carry, half=half, side=side, step=step, offset=offset, me=me):
+                second, block = lax.div(index, OWN), lax.rem(index, OWN)
+                own = piece(half, wrap(me + step), second + offset)[block]
+                got = relay[half, side, second, block]
+                forward[half, side, second, block] = (own.astype(jnp.float32) + got.astype(jnp.float32)).astype(
+                    jnp.bfloat16
+                )
+                return carry
+
+            lax.fori_loop(0, 2 * OWN, add_relay, 0)
+            last = copy(4 + side, half, 0, step, forward.at[half, side], message.at[half, side, pl.ds(offset, 2)])
+            last.start()
+            first_copies[half].append(last)
+
+    second_copies = [[], []]
+    for half in range(2):
+        for number in range(2, 6):
+            first_copies[half][number].wait_recv()
+        me, other = places[half]
+
+        def add_first(index, carry, half=half, me=me):
+            second, block = lax.div(index, OWN), lax.rem(index, OWN)
+            value = piece(half, me, second)[block].astype(jnp.float32)
+            value += message[half, 0, second, block].astype(jnp.float32)
+            value += message[half, 1, second, block].astype(jnp.float32)
+            reduced[half, second, block] = value.astype(jnp.bfloat16)
+            return carry
+
+        lax.fori_loop(0, 4 * OWN, add_first, 0)
+        there, after, before = wrap(other + 2), wrap(other + 1), wrap(other - 1)
+        low3, high3 = pl.ds(0, 3), pl.ds(3, 3)
+        batch = [
+            copy(0, half, 1, 1, reduced.at[half, there, low3], relay2.at[half, 0]),
+            copy(1, half, 1, -1, reduced.at[half, there, high3], relay2.at[half, 1]),
+            copy(2, half, 1, 1, reduced.at[half, after, high3], message2.at[half, 0, high3]),
+            copy(3, half, 1, -1, reduced.at[half, before, low3], message2.at[half, 1, low3]),
+        ]
+        for item in batch:
+            item.start()
+        second_copies[half] = batch
+
+    for half in range(2):
+        other = places[half][1]
+        for side, step, offset in ((0, 1, 0), (1, -1, 3)):
+            second_copies[half][side].wait_recv()
+            target = wrap(other + step)
+            for block in range(3):
+                own = reduced[half, target, block + offset].astype(jnp.float32)
+                got = relay2[half, side, block].astype(jnp.float32)
+                forward2[half, side, block] = (own + got).astype(jnp.bfloat16)
+            last = copy(4 + side, half, 1, step, forward2.at[half, side], message2.at[half, side, pl.ds(offset, 3)])
+            last.start()
+            second_copies[half].append(last)
+
+    for half in range(2):
+        other = places[half][1]
+        for number in range(2, 6):
+            second_copies[half][number].wait_recv()
+        for block in range(OWN):
+            value = reduced[half, other, block].astype(jnp.float32)
+            value += message2[half, 0, block].astype(jnp.float32)
+            value += message2[half, 1, block].astype(jnp.float32)
+            out[block * BLOCK : (block + 1) * BLOCK, half * 128 : half * 128 + 128] = value.T
+
+    for half in range(2):
+        for item in first_copies[half] + second_copies[half]:
+            item.wait_send()
+
+
+def owner_sums(sums):
+    vmem = pl.BlockSpec(memory_space=pltpu.VMEM)
+    tile = (WIN // 2, BLOCK)
+    return pl.pallas_call(
+        reduce_kernel,
+        out_shape=jax.ShapeDtypeStruct((OWN * BLOCK, WIN), jnp.float32),
+        in_specs=[vmem],
+        out_specs=vmem,
+        scratch_shapes=[
+            pltpu.VMEM((2, 2, 2, OWN, *tile), jnp.bfloat16),
+            pltpu.VMEM((2, 2, 4, OWN, *tile), jnp.bfloat16),
+            pltpu.VMEM((2, 2, 2, OWN, *tile), jnp.bfloat16),
+            pltpu.VMEM((2, 4, OWN, *tile), jnp.bfloat16),
+            pltpu.VMEM((2, 2, 3, *tile), jnp.bfloat16),
+            pltpu.VMEM((2, 2, OWN, *tile), jnp.bfloat16),
+            pltpu.VMEM((2, 2, 3, *tile), jnp.bfloat16),
+            pltpu.SemaphoreType.DMA((2, 2, 6)),
+            pltpu.SemaphoreType.DMA((2, 2, 6)),
+        ],
+        compiler_params=pltpu.CompilerParams(
+            collective_id=1, has_side_effects=True, vmem_limit_bytes=40 * 1024 * 1024
+        ),
+    )(sums)
 
 
 def directions(angles):
@@ -201,12 +348,7 @@
     packed, counts = entry_codes(sources, offsets, table, line)
     sums = partial_sums(packed.reshape(-1), counts, dirs.reshape(-1), toward, geometry, signals)
 
-    sums = sums.reshape(NZ, NY, OWN, WIN, BLOCK)
-    sums = lax.all_to_all(sums, "y", split_axis=1, concat_axis=1, tiled=True)
-    sums = jnp.sum(sums.astype(jnp.float32), axis=1).astype(jnp.bfloat16)
-    sums = lax.all_to_all(sums, "z", split_axis=0, concat_axis=0, tiled=True)
-    sums = jnp.sum(sums.astype(jnp.float32), axis=0)
-    return sums.transpose(0, 2, 1).reshape(OWN * BLOCK, WIN)
+    return owner_sums(sums.reshape(2, NZ, NY, OWN, WIN // 2, BLOCK))
 
 
 def solution(mesh):

time: 287 us -> 225 us (0.78)
  blocking collectives: 102 us -> 0 us
  Pallas kernels: 46.1 us -> 91.5 us
  other arithmetic: 15.9 us -> 11.5 us
    all_to_all x2 -> x0, blocking collectives: 102 us -> none  [the longest x1 74.2 us: body(): sums = lax.all_to_all(sums, 'y', split_axis=1, concat_axis=1, tiled=True)]
    pallas_call x1 -> x2, Pallas kernels: 46.1 us -> 91.5 us  [the longest x1 46.9 us: owner_sums(): pl.pallas_call(reduce_kernel, out_shape=jax.ShapeDtypeStruct((OWN * BLOCK...]
    reduce_sum x2 -> x0, other arithmetic: 4.38 us -> none  [the longest x1 4.14 us: body(): sums = jnp.sum(sums.astype(jnp.float32), axis=1).astype(jnp.bfloat16)]
    unnamed x15 -> x18, local copies, waits for them, and re-layouts: 8.51 us -> 12.2 us
    reshape x1 -> x0, local copies, waits for them, and re-layouts: 3.21 us -> none  [body(): sums = sums.reshape(NZ, NY, OWN, WIN, BLOCK)]
  transfers between devices with their start and end apart: 6 -> 6, of which waited for: 3 -> 3; matrix products, arithmetic and copies ran while one was open for 9% -> 11% of each run, Pallas kernels for 0% -> 0%
where the time goes in v2:
time: 225 us; the launch traced here: 224 us
  Pallas kernels  91.5 us (41%)
  waiting for transfers between devices  65.1 us (29%)
  local copies, waits for them, and re-layouts  29.4 us (13%)
  between operations  15.8 us (7%)
  other arithmetic  11.5 us (5%)
  starting transfers between devices  10.6 us (5%)
    unnamed x3, waiting for transfers between devices  63.5 us
    pallas_call x1, Pallas kernels, owner_sums(): pl.pallas_call(reduce_kernel, out_shape=jax.ShapeDtypeStruct((OWN * BLOCK...  46.9 us
    pallas_call x1, Pallas kernels, partial_sums(): pl.pallas_call(partial_kernel, out_shape=jax.ShapeDtypeStruct((2, ROWS, W...  44.6 us
    unnamed x18, local copies, waits for them, and re-layouts  12.2 us
    slice x1, local copies, waits for them, and re-layouts, body(): signals = gathered[:, :BLOCKS_HERE * BUF].reshape(SLOTS, BUF, 2 * BLOCK)  7.17 us
    ppermute x1, starting transfers between devices, filter_local(): high = lax.ppermute(framed[:1], AZI, back)  5.7 us
  transfers between devices with their start and end apart: 6, of which 3 were waited for; matrix products, arithmetic and copies ran while one was open for 11% of the time, Pallas kernels for 0%

profile of v2, /device:TPU:0, one launch (start us, length us, event | category | flops | bytes accessed | tf_op | source)
XLA Modules:
  0.0 223.9 jit_solution(4625222317497489882)
XLA Ops:
  7.4 1.0 fusion.11
  8.3 3.5 %collective-permute-start = (bf16[32,1,2,512]{3,2,1,0:T(2,128)(2,1)S(1)}, bf16[32,1,2,512]{3,2,1,0:T(2,128)(2,1)S(1)}, u32[]{:S(2)}, u32[]{:S(2)}) collective-permute-start(bf16[32,1,2,512]{3,2,1,0:T(2,128)(2,1)S(1)} %get-tuple-element.12), channel_id=1, source_target_pairs={{0,1},{1,2},{2,3},{4,5},{5,6},{6,7},{8,9},{9,10},{10,11},{12,13},{... | collective-permute-start | bytes 196616 | tf_op jit(solution)/shard_map/ppermute | solution.py:32
  11.8 1.3 collective-permute-start.1
  13.1 0.7 reshape.141
  13.9 0.7 convert_element_type.40
  14.6 0.7 convert_element_type.41
  15.4 0.8 copy.59
  16.2 1.2 dynamic-slice
  18.2 0.3 dynamic-update-slice
  18.6 0.7 copy-done.1
  19.3 0.8 copy.63
  20.1 0.1 concatenate.28
  20.2 0.8 copy.64
  21.0 0.1 concatenate.29
  21.1 0.8 copy.65
  21.9 0.1 concatenate.30
  22.1 0.7 convert_bitcast_fusion
  22.9 2.6 %constant_dynamic-update-slice_fusion.1 = bf16[32,18,2,512]{3,2,1,0:T(2,128)(2,1)S(1)} fusion(bf16[32,18,2,512]{3,2,1,0:T(2,128)(2,1)S(1)} %constant_dynamic-update-slice_fusion.2, bf16[32,16,2,512]{3,2,1,0:T(2,128)(2,1)} %param.9), kind=kLoop, calls=%fused_computation.25 | loop fusion | bytes 2097152
  25.6 5.7 %collective-permute-start.3 = (bf16[1,18,2,512]{3,2,1,0:T(2,128)(2,1)S(1)}, bf16[1,18,2,512]{3,2,1,0:T(2,128)(2,1)S(1)}, u32[]{:S(2)}, u32[]{:S(2)}) collective-permute-start(bf16[1,18,2,512]{3,2,1,0:T(2,128)(2,1)S(1)} %get-tuple-element.10), channel_id=1, source_target_pairs={{4,0},{8,4},{12,8},{16,12},{20,16},{24,20},{28,24},{32,28},{36,32}... | collective-permute-start | bytes 110600 | tf_op jit(solution)/shard_map/ppermute | solution.py:39
  31.4 1.5 collective-permute-done.2
  33.0 1.6 maximum_convert_fusion
  34.6 3.3 %fusion = f32[32,18,2,512]{3,2,1,0:T(2,128)S(1)} fusion(f32[34,18,2,512]{3,2,1,0:T(2,128)S(1)} %maximum_convert_fusion), kind=kLoop, calls=%fused_computation.1 | loop fusion | flops 2359296 | bytes 9437184 | tf_op jit(solution)/shard_map/mul | solution.py:41
  37.9 2.3 %fusion.4 = bf16[32,16,2,512]{3,2,1,0:T(2,128)(2,1)S(1)} fusion(f32[32,18,2,512]{3,2,1,0:T(2,128)S(1)} %fusion), kind=kLoop, calls=%fused_computation.8 | loop fusion | flops 2621440 | bytes 7340032 | tf_op jit(solution)/shard_map/convert_element_type | solution.py:43
  40.2 1.5 copy.62
  41.7 0.1 copy.80
  41.9 1.1 fusion.6
  43.1 63.5 %all-reduce.4.cloned.1.call-done = f32[43200]{0:T(1024)} async-done(((f32[43200]{0:T(1024)}), f32[43200]{0:T(1024)}) %all-reduce.4.cloned.1.call-update) | async-done | bytes 172816
  106.5 1.1 reshape.164
  108.1 0.1 mul.82
  108.2 0.1 copy.72
  108.6 0.1 broadcast_in_dim.44
  108.8 0.1 fusion.7
  108.9 0.6 reduce_sum.32.toward
  109.6 0.8 reshape.157.dirs
  110.3 0.1 select_reduce_fusion
  110.4 0.9 slice_bitcast_fusion
  111.5 7.2 %slice.102 = bf16[8,2048,256]{2,1,0:T(8,128)(2,1)} slice(bf16[8,2080,256]{2,1,0:T(8,128)(2,1)} %bitcast.41), slice={[0:8], [0:2048], [0:256]} | slice | bytes 16777216 | tf_op jit(solution)/shard_map/slice | solution.py:341
  118.7 0.1 copy.67
  118.9 0.1 reshape.154
  119.1 0.1 broadcast_in_dim.52
  119.2 0.5 convert_reduce_fusion
  119.8 0.1 copy.69
  119.9 0.7 reshape.155.codes
  120.6 0.7 reshape.163.geometry
  121.3 44.6 %shard_map.91 = bf16[2,96,128,128]{3,2,1,0:T(8,128)(2,1)} custom-call(s32[768]{0:T(1024)} %reshape.155.codes, s32[96]{0:T(128)} %get-tuple-element.5.counts, f32[288]{0:T(512)} %reshape.157.dirs, f32[96,128]{1,0:T(8,128)} %reduce_sum.32.toward, f32[32,8,128]{2,1,0:T(8,128)} %reshape.163.geometry, bf16[32,512,256]{2,1,0:T(8,128)(2,1)} %bitcast.39), custom_call_target="tpu_custom_call" | custom-call | tf_op jit(solution)/shard_map/pallas_call | solution.py:133
  165.8 2.8 %copy-done = bf16[2,96,128,128]{3,2,1,0:T(8,128)(2,1)S(1)} copy-done((bf16[2,96,128,128]{3,2,1,0:T(8,128)(2,1)S(1)}, bf16[2,96,128,128]{3,2,1,0:T(8,128)(2,1)}, u32[]{:S(2)}) %copy-start) | copy-done | bytes 6291480
  168.6 46.9 %shard_map.92 = f32[768,256]{1,0:T(8,128)S(1)} custom-call(bf16[2,4,4,6,128,128]{5,4,3,2,1,0:T(8,128)(2,1)S(1)} %bitcast.38), custom_call_target="tpu_custom_call" | custom-call | tf_op jit(solution)/shard_map/pallas_call | solution.py:272
  215.6 0.9 copy.87
  (55 shorter events, 2.2 us)
Async XLA Ops:
  7.4 99.2 %all-reduce.4.cloned.1.call-start = ((), (), s32[]{:S(2)}) async-start(), calls=%async_computation.1 | async-start | bytes 352256
  8.3 14.5 %collective-permute-start = (bf16[32,1,2,512]{3,2,1,0:T(2,128)(2,1)S(1)}, bf16[32,1,2,512]{3,2,1,0:T(2,128)(2,1)S(1)}, u32[]{:S(2)}, u32[]{:S(2)}) collective-permute-start(bf16[32,1,2,512]{3,2,1,0:T(2,128)(2,1)S(1)} %get-tuple-element.12), channel_id=1, source_target_pairs={{0,1},{1,2},{2,3},{4,5},{5,6},{6,7},{8,9},{9,10},{10,11},{12,13},{... | collective-permute-start | bytes 196616 | tf_op jit(solution)/shard_map/ppermute | solution.py:32
  11.8 13.6 %collective-permute-start.1 = (bf16[32,1,2,512]{3,2,1,0:T(2,128)(2,1)S(1)}, bf16[32,1,2,512]{3,2,1,0:T(2,128)(2,1)S(1)}, u32[]{:S(2)}, u32[]{:S(2)}) collective-permute-start(bf16[32,1,2,512]{3,2,1,0:T(2,128)(2,1)S(1)} %get-tuple-element.11), channel_id=1, source_target_pairs={{1,0},{2,1},{3,2},{5,4},{6,5},{7,6},{9,8},{10,9},{11,10},{13,12},{... | collective-permute-start | bytes 196616 | tf_op jit(solution)/shard_map/ppermute | solution.py:33
  18.6 0.7 copy-start.1
  19.3 91.2 %all-gather.4.cloned.1.call-start = ((), (), s32[]{:S(2)}) async-start(), calls=%async_computation | async-start | bytes 9584640 | tf_op jit(solution)/shard_map/all_gather | solution.py:340
  25.6 7.3 %collective-permute-start.2 = (bf16[1,18,2,512]{3,2,1,0:T(2,128)(2,1)S(1)}, bf16[1,18,2,512]{3,2,1,0:T(2,128)(2,1)S(1)}, u32[]{:S(2)}, u32[]{:S(2)}) collective-permute-start(bf16[1,18,2,512]{3,2,1,0:T(2,128)(2,1)S(1)} %get-tuple-element.9), channel_id=1, source_target_pairs={{0,4},{4,8},{8,12},{12,16},{16,20},{20,24},{24,28},{28,32},{32,36}... | collective-permute-start | bytes 110600 | tf_op jit(solution)/shard_map/ppermute | solution.py:38
  25.6 7.3 %collective-permute-start.3 = (bf16[1,18,2,512]{3,2,1,0:T(2,128)(2,1)S(1)}, bf16[1,18,2,512]{3,2,1,0:T(2,128)(2,1)S(1)}, u32[]{:S(2)}, u32[]{:S(2)}) collective-permute-start(bf16[1,18,2,512]{3,2,1,0:T(2,128)(2,1)S(1)} %get-tuple-element.10), channel_id=1, source_target_pairs={{4,0},{8,4},{12,8},{16,12},{20,16},{24,20},{28,24},{32,28},{36,32}... | collective-permute-start | bytes 110600 | tf_op jit(solution)/shard_map/ppermute | solution.py:39
  165.8 2.8 %copy-start = (bf16[2,96,128,128]{3,2,1,0:T(8,128)(2,1)S(1)}, bf16[2,96,128,128]{3,2,1,0:T(8,128)(2,1)}, u32[]{:S(2)}) copy-start(bf16[2,96,128,128]{3,2,1,0:T(8,128)(2,1)} %shard_map.91) | copy-start | bytes 18874372
Sparse Core Ops, SparseCore 0:
  19.4 87.1 all-reduce.3
Sparse Core Ops, SparseCore 1:
  43.1 52.4 all-gather.3

commit v3 on v2

--- a/solution.py
+++ b/solution.py
@@ -12,6 +12,8 @@
 WIN = 256
 BUF = 512
 BLOCKS_HERE = 4
+AXL = 16
+AZL = 32
 OWN = 6
 NZ, NY, NC, NX = 4, 4, 2, 4
 LINES = NZ * NY
@@ -25,22 +27,179 @@
 MESH = pl.DeviceIdType.MESH
 
 
-def filter_local(surface_data):
-    count = lax.axis_size("ax")
-    up = [(i, i + 1) for i in range(count - 1)]
-    down = [(b, a) for a, b in up]
-    low = lax.ppermute(surface_data[:, -1:], "ax", up)
-    high = lax.ppermute(surface_data[:, :1], "ax", down)
-    framed = jnp.concatenate([low, surface_data, high], axis=1)
-    count = NZ * NY * NC
-    ring = [(i, (i + 1) % count) for i in range(count)]
-    back = [(b, a) for a, b in ring]
-    low = lax.ppermute(framed[-1:], AZI, ring)
-    high = lax.ppermute(framed[:1], AZI, back)
-    widened = jnp.concatenate([low, framed, high], axis=0).astype(jnp.float32)
-    passed = 0.25 * (widened[:-2] + 2.0 * widened[1:-1] + widened[2:])
-    filtered = 0.25 * (passed[:, :-2] + 2.0 * passed[:, 1:-1] + passed[:, 2:])
-    return filtered.astype(jnp.bfloat16)
+def wrap(index):
+    return lax.rem(index + 4, 4)
+
+
+def gather_kernel(
+    surface, edges, small, obs_pos, dirs, sources, offsets,
+    signals, asked,
+    own, own_asked, row_halo, col_halo, corners, edge_pass, smooth,
+    send, recv, local,
+):
+    z, y = lax.axis_index("z"), lax.axis_index("y")
+    core, ax = lax.axis_index("core"), lax.axis_index("ax")
+    line = z * NY + y
+    azimuth = line * NC + core
+    unit = core * NX + ax
+
+    def azi_device(index):
+        index = lax.rem(index + NZ * NY * NC, NZ * NY * NC)
+        return {"z": index // (NY * NC), "y": lax.rem(index // NC, NY), "core": lax.rem(index, NC)}
+
+    following, preceding = azi_device(azimuth + 1), azi_device(azimuth - 1)
+    right, left = {"ax": wrap(ax + 1)}, {"ax": wrap(ax - 1)}
+    sibling = {"core": 1 - core}
+    plane = [{"z": wrap(z + k // NY), "y": wrap(y + k % NY)} for k in range(1, LINES)]
+
+    barrier = pltpu.get_barrier_semaphore()
+    for device in [following, preceding, right, left] + plane:
+        pl.semaphore_signal(barrier, inc=1, device_id=device, device_id_type=MESH)
+    pl.semaphore_wait(barrier, 4 + len(plane))
+
+    started = []
+
+    def push(src, dst, device):
+        number = len(started)
+        item = pltpu.make_async_remote_copy(
+            src_ref=src,
+            dst_ref=dst,
+            send_sem=send.at[number],
+            recv_sem=recv.at[number],
+            device_id=device,
+            device_id_type=MESH,
+        )
+        item.start()
+        started.append(item)
+        return item
+
+    col_low = push(edges.at[1], col_halo.at[0], right)
+    col_high = push(edges.at[0], col_halo.at[1], left)
+    row_low = push(surface.at[AZL - 1], row_halo.at[0], following)
+    row_high = push(surface.at[0], row_halo.at[1], preceding)
+
+    own_asked[...] = jnp.zeros_like(own_asked)
+    for index in range(3 * OWN):
+        part, block = divmod(index, OWN)
+        own_asked[index : index + 1, :] = obs_pos[part : part + 1, block * BLOCK : (block + 1) * BLOCK]
+    own_asked[24 : 24 + OWN, 0:32] = sources[...].astype(jnp.float32)
+    own_asked[32 : 32 + OWN, 0:32] = offsets[...].astype(jnp.float32)
+    own_asked[40:43, 0:OWN] = dirs[...]
+    own[BLOCKS_HERE * BUF :, :] = small[...]
+
+    col_low.wait_recv()
+    col_high.wait_recv()
+    corner_low = push(col_halo.at[:, pl.ds(16, 16)], corners.at[0], following)
+    corner_high = push(col_halo.at[:, pl.ds(0, 16)], corners.at[1], preceding)
+    row_low.wait_recv()
+    row_high.wait_recv()
+    corner_low.wait_recv()
+    corner_high.wait_recv()
+    tables = [push(own_asked, asked.at[line], device) for device in plane]
+    keep_asked = pltpu.make_async_copy(own_asked, asked.at[line], local.at[4])
+    keep_asked.start()
+
+    row32 = lax.broadcasted_iota(jnp.int32, (AZL, 2 * BUF), 0)
+    for side in range(2):
+        mid = col_halo[side].astype(jnp.float32)
+        above = jnp.where(row32 == 0, corners[0, side, 15:16, :].astype(jnp.float32), pltpu.roll(mid, 1, 0))
+        below = jnp.where(row32 == AZL - 1, corners[1, side, 0:1, :].astype(jnp.float32), pltpu.roll(mid, AZL - 1, 0))
+        there = (ax > 0) if side == 0 else (ax < NX - 1)
+        edge_pass[side] = jnp.where(there, 0.25 * (above + 2.0 * mid + below), 0.0)
+
+    chunks = [(0, BUF), (BUF, BUF), (2 * BUF, BUF), (3 * BUF, BUF + 32)]
+    row16 = lax.broadcasted_iota(jnp.int32, (AXL, 2 * BUF), 0)
+    to_right, to_left, to_sibling, kept = {}, {}, {}, []
+
+    def region(owner_core, owner_ax, chunk):
+        start, size = chunks[chunk]
+        return signals.at[owner_core * NX + owner_ax, pl.ds(start, size)]
+
+    def make_block(block):
+        for part in range(8):
+            row = block * 8 + part
+            above = row_halo[0] if row == 0 else surface[row - 1]
+            below = row_halo[1] if row == AZL - 1 else surface[row + 1]
+            passed = 0.25 * (
+                above.astype(jnp.float32) + 2.0 * surface[row].astype(jnp.float32) + below.astype(jnp.float32)
+            )
+            before = jnp.where(row16 == 0, edge_pass[0, row : row + 1, :], pltpu.roll(passed, 1, 0))
+            after = jnp.where(row16 == AXL - 1, edge_pass[1, row : row + 1, :], pltpu.roll(passed, AXL - 1, 0))
+            smooth[part * 16 : part * 16 + 16, :] = 0.25 * (before + 2.0 * passed + after)
+        for channel in range(2):
+            for part in range(4):
+                tile = smooth[:, channel * BUF + part * 128 : channel * BUF + part * 128 + 128]
+                own[
+                    block * BUF + part * 128 : block * BUF + part * 128 + 128, channel * 128 : channel * 128 + 128
+                ] = tile.T.astype(jnp.bfloat16)
+
+    for chunk in range(4):
+        make_block(chunk)
+        start, size = chunks[chunk]
+        mine = own.at[pl.ds(start, size)]
+        to_right[chunk] = push(mine, region(core, ax, chunk), right)
+        to_left[chunk] = push(mine, region(core, ax, chunk), left)
+        to_sibling[chunk] = push(mine, region(core, ax, chunk), sibling)
+        keep = pltpu.make_async_copy(mine, region(core, ax, chunk), local.at[chunk])
+        keep.start()
+        kept.append(keep)
+
+    later = []
+    for chunk in range(4):
+        to_right[chunk].wait_recv()
+        came = region(core, wrap(ax - 1), chunk)
+        if chunk < 2:
+            later.append((push(came, came, right), wrap(ax - 2), chunk))
+        to_sibling[chunk + 10] = push(came, came, sibling)
+        to_left[chunk].wait_recv()
+        came = region(core, wrap(ax + 1), chunk)
+        if chunk >= 2:
+            later.append((push(came, came, left), wrap(ax + 2), chunk))
+        to_sibling[chunk + 20] = push(came, came, sibling)
+    for item, opposite, chunk in later:
+        item.wait_recv()
+        came = region(core, opposite, chunk)
+        to_sibling[chunk + 30] = push(came, came, sibling)
+    for item in to_sibling.values():
+        item.wait_recv()
+    for item in tables:
+        item.wait_recv()
+    keep_asked.wait()
+    for item in kept:
+        item.wait()
+    for item in started:
+        item.wait_send()
+
+
+def gather(surface, edges, small, obs_pos, dirs, sources, offsets):
+    vmem = pl.BlockSpec(memory_space=pltpu.VMEM)
+    anywhere = pl.BlockSpec(memory_space=pl.ANY)
+    copies = 6 + (LINES - 1) + 12 + 8 + 4 + 4
+    rows = BLOCKS_HERE * BUF + 32
+    return pl.pallas_call(
+        gather_kernel,
+        out_shape=(
+            jax.ShapeDtypeStruct((GROUP, rows, 2 * BLOCK), jnp.bfloat16),
+            jax.ShapeDtypeStruct((LINES, 48, 128), jnp.float32),
+        ),
+        in_specs=[vmem] * 7,
+        out_specs=(anywhere, anywhere),
+        scratch_shapes=[
+            pltpu.VMEM((rows, 2 * BLOCK), jnp.bfloat16),
+            pltpu.VMEM((48, 128), jnp.float32),
+            pltpu.VMEM((2, AXL, 2 * BUF), jnp.bfloat16),
+            pltpu.VMEM((2, AZL, 2 * BUF), jnp.bfloat16),
+            pltpu.VMEM((2, 2, 16, 2 * BUF), jnp.bfloat16),
+            pltpu.VMEM((2, AZL, 2 * BUF), jnp.float32),
+            pltpu.VMEM((BLOCK, 2 * BUF), jnp.float32),
+            pltpu.SemaphoreType.DMA((copies,)),
+            pltpu.SemaphoreType.DMA((copies,)),
+            pltpu.SemaphoreType.DMA((5,)),
+        ],
+        compiler_params=pltpu.CompilerParams(
+            collective_id=2, has_side_effects=True, vmem_limit_bytes=40 * 1024 * 1024
+        ),
+    )(surface, edges, small, obs_pos, dirs, sources, offsets)
 
 
 def entry_codes(sources, offsets, table, line):
@@ -59,7 +218,8 @@
 
 def partial_kernel(codes, counts, dirs, toward, geometry, signals, out, source, weights, total, reach_obs):
     def build(slot, carry):
-        level = signals[slot].astype(jnp.float32)
+        rows = pl.ds(pl.multiple_of(lax.rem(slot, BLOCKS_HERE) * BUF, BUF), BUF)
+        level = signals[lax.div(slot, BLOCKS_HERE), rows, :].astype(jnp.float32)
         slope = 0.5 * (pltpu.roll(level, BUF - 1, 0) - pltpu.roll(level, 1, 0))
         slope = slope.astype(jnp.bfloat16).astype(jnp.float32)
         source[slot * 3, 0:BUF, :] = slope[:, 128:256]
@@ -146,10 +306,6 @@
     )(codes, counts, dirs, toward, geometry, signals)
 
 
-def wrap(index):
-    return lax.rem(index + 4, 4)
-
-
 def reduce_kernel(sums, out, relay, message, forward, reduced, relay2, message2, forward2, send, recv):
     z, y = lax.axis_index("z"), lax.axis_index("y")
     axes = (("y", "z"), ("z", "y"))
@@ -311,35 +467,22 @@
     core, ax = lax.axis_index("core"), lax.axis_index("ax")
     line = z * NY + y
 
-    asked = jnp.concatenate(
-        [
-            obs_pos.reshape(-1),
-            obs_angles.T.reshape(-1),
-            entry_source.astype(jnp.float32).reshape(-1),
-            entry_offset.astype(jnp.float32).reshape(-1),
-        ]
-    )
-    asked = lax.all_gather(asked, ("z", "y"))
-    n_pos, n_ang, n_ent = 3 * OWN * BLOCK, 2 * OWN, OWN * 32
-    pos = asked[:, :n_pos].reshape(LINES, 3, OWN, BLOCK).transpose(0, 2, 1, 3).reshape(ROWS, 3, BLOCK)
-    dirs = directions(asked[:, n_pos : n_pos + n_ang].reshape(ROWS, 2))
-    entries = asked[:, n_pos + n_ang :].astype(jnp.int32)
-    sources = entries[:, :n_ent].reshape(ROWS, 32)
-    offsets = entries[:, n_ent:].reshape(ROWS, 32)
-    toward = jnp.sum(dirs[:, :, None] * pos, axis=1)
-
-    filtered = filter_local(surface_data)
-    panels = filtered.reshape(BLOCKS_HERE, BLOCK, 2, BUF).transpose(0, 3, 2, 1).reshape(-1, 2 * BLOCK)
+    surface = surface_data.reshape(AZL, AXL, 2 * BUF)
+    edges = jnp.stack([surface[:, 0], surface[:, AXL - 1]], 0)
     geometry = jnp.concatenate(
         [panel_pos, panel_normal, panel_area[None], jnp.zeros_like(panel_area)[None]], 0
     ).reshape(8, BLOCKS_HERE, BLOCK).transpose(1, 0, 2)
-    listed = send_list.astype(jnp.bfloat16)
-    small = jnp.concatenate([geometry.reshape(-1), listed.reshape(-1), jnp.zeros((128,), jnp.bfloat16)])
-    small_rows = small.shape[0] // 256
-    small = jnp.pad(small.reshape(small_rows, 256), ((0, 32 - small_rows), (0, 0)))
-    gathered = lax.all_gather(jnp.concatenate([panels, small], 0), ("core", "ax"))
-    signals = gathered[:, : BLOCKS_HERE * BUF].reshape(SLOTS, BUF, 2 * BLOCK)
-    small = gathered[:, BLOCKS_HERE * BUF :].reshape(GROUP, -1)
+    small = jnp.concatenate([geometry.reshape(-1), send_list.astype(jnp.bfloat16).reshape(-1)])
+    small = jnp.pad(small, (0, 32 * 256 - small.shape[0])).reshape(32, 256)
+    signals, asked = gather(
+        surface, edges, small, obs_pos, directions(obs_angles.T).T, entry_source, entry_offset
+    )
+    pos = asked[:, : 3 * OWN].reshape(LINES, 3, OWN, BLOCK)
+    dirs = asked[:, 40:43, :OWN].transpose(0, 2, 1)
+    sources = asked[:, 24 : 24 + OWN, :32].astype(jnp.int32).reshape(ROWS, 32)
+    offsets = asked[:, 32 : 32 + OWN, :32].astype(jnp.int32).reshape(ROWS, 32)
+    toward = jnp.sum(dirs.transpose(0, 2, 1)[..., None] * pos, axis=1).reshape(ROWS, BLOCK)
+    small = signals[:, BLOCKS_HERE * BUF :].reshape(GROUP, -1)
     geometry = small[:, : BLOCKS_HERE * 8 * BLOCK].reshape(SLOTS, 8, BLOCK).astype(jnp.float32)
     listed = small[:, BLOCKS_HERE * 8 * BLOCK : BLOCKS_HERE * 8 * BLOCK + 128].astype(jnp.int32)
     table = listed.reshape(GROUP, LINES, NC, NX)

time: 225 us -> 165 us (0.73)
  waiting for transfers between devices: 65.1 us -> 0 us
  Pallas kernels: 91.5 us -> 141 us
  between operations: 15.8 us -> 0.22 us
  local copies, waits for them, and re-layouts: 29.4 us -> 18.7 us
  starting transfers between devices: 10.6 us -> 0 us
  other arithmetic: 11.5 us -> 2.52 us
    unnamed x3 -> x0, waiting for transfers between devices: 63.5 us -> none
    pallas_call x0 -> x1, Pallas kernels: none -> 53.6 us  [gather(): pl.pallas_call(gather_kernel, out_shape=(jax.ShapeDtypeStruct((GROUP, row...]
    ppermute x4 -> x0, starting transfers between devices: 10.5 us -> none  [the longest x1 5.7 us: filter_local(): high = lax.ppermute(framed[:1], AZI, back)]
    slice x7 -> x6, local copies, waits for them, and re-layouts: 8.35 us -> 0.36 us  [the longest x1 0.21 us: body(): edges = jnp.stack([surface[:, 0], surface[:, AXL - 1]], 0)]
    pallas_call x1, Pallas kernels: 46.9 us -> 39.2 us  [owner_sums(): pl.pallas_call(reduce_kernel, out_shape=jax.ShapeDtypeStruct((OWN * BLOCK...]
    convert_element_type x5 -> x1, other arithmetic: 5.39 us -> 0.01 us  [body(): sources = asked[:, 24:24 + OWN, :32].astype(jnp.int32).reshape(ROWS, 32)]
    pallas_call x1, Pallas kernels: 44.6 us -> 48.5 us  [partial_sums(): pl.pallas_call(partial_kernel, out_shape=jax.ShapeDtypeStruct((2, ROWS, W...]
    mul x1 -> x0, other arithmetic: 3.27 us -> none  [filter_local(): passed = 0.25 * (widened[:-2] + 2.0 * widened[1:-1] + widened[2:])]
  transfers between devices with their start and end apart: 6 -> 0, of which waited for: 3 -> 0; matrix products, arithmetic and copies ran while one was open for 11% -> 0% of each run, Pallas kernels for 0% -> 0%
where the time goes in v3:
time: 165 us; the launch traced here: 163 us
  Pallas kernels  141 us (85%)
  local copies, waits for them, and re-layouts  18.7 us (11%)
  other arithmetic  2.52 us (2%)
    pallas_call x1, Pallas kernels, gather(): pl.pallas_call(gather_kernel, out_shape=(jax.ShapeDtypeStruct((GROUP, row...  53.6 us
    pallas_call x1, Pallas kernels, partial_sums(): pl.pallas_call(partial_kernel, out_shape=jax.ShapeDtypeStruct((2, ROWS, W...  48.5 us
    pallas_call x1, Pallas kernels, owner_sums(): pl.pallas_call(reduce_kernel, out_shape=jax.ShapeDtypeStruct((OWN * BLOCK...  39.2 us
    unnamed x17, local copies, waits for them, and re-layouts  12.5 us

profile of v3, /device:TPU:0, one launch (start us, length us, event | category | flops | bytes accessed | tf_op | source)
XLA Modules:
  0.0 162.8 jit_solution(14499632006366049714)
XLA Ops:
  0.0 0.7 convert_bitcast_fusion
  0.7 0.1 pad.13.clone
  0.7 0.8 cosine_multiply_fusion
  1.6 0.8 copy.46
  2.3 0.1 concatenate.15
  2.4 0.8 copy.44
  3.2 0.1 concatenate.13
  3.3 0.8 copy.45
  4.1 0.1 concatenate.14
  4.2 0.1 maximum_bitcast_fusion
  4.3 1.8 %reshape.136.surface = bf16[32,16,1024]{2,1,0:T(8,128)(2,1)S(1)} reshape(bf16[32,16,2,512]{3,2,1,0:T(2,128)(2,1)} %param.9) | data formatting | bytes 2097152 | tf_op jit(solution)/shard_map/reshape | solution.py:470
  6.1 0.2 fusion.5
  6.4 0.0 copy-start.2
  6.4 0.7 copy-done.2
  7.1 0.0 copy-start.3
  7.1 0.7 copy-done.3
  7.8 0.0 copy-start.4
  7.8 0.7 copy-done.4
  8.5 53.6 %shard_map.91 = (bf16[8,2080,256]{2,1,0:T(8,128)(2,1)S(1)}, f32[16,48,128]{2,1,0:T(8,128)S(1)}) custom-call(bf16[32,16,1024]{2,1,0:T(8,128)(2,1)S(1)} %reshape.136.surface, bf16[2,32,1024]{2,1,0:T(8,128)(2,1)S(1)} %pad_maximum_fusion.edges, bf16[32,256]{1,0:T(8,128)(2,1)S(1)} %reshape.122.small, f32[3,768]{1,0:T(4,128)S(1)} %copy-done.2, ...), custom_call_target="tpu_custom_call" | custom-call | tf_op jit(solution)/shard_map/pallas_call | solution.py:179
  62.1 0.0 copy-start.1
  62.1 3.3 %copy-done.1 = bf16[8,2080,256]{2,1,0:T(8,128)(2,1)} copy-done((bf16[8,2080,256]{2,1,0:T(8,128)(2,1)}, bf16[8,2080,256]{2,1,0:T(8,128)(2,1)S(1)}, u32[]{:S(2)}) %copy-start.1) | copy-done | bytes 8519704
  65.4 0.1 copy.55
  65.5 0.2 copy.54
  65.7 0.8 reshape.129.dirs
  66.4 0.9 slice_bitcast_fusion
  67.4 0.1 copy.62
  67.5 0.7 reshape.135.geometry
  68.2 0.1 copy.61
  68.3 0.1 copy.52
  68.4 0.1 broadcast_in_dim.47
  68.5 0.1 broadcast_in_dim.48
  68.6 0.1 broadcast_in_dim.44
  68.6 0.1 reshape.127
  68.8 0.1 multiply_reduce_fusion
  69.0 0.1 copy.49
  69.1 0.6 reshape.131.toward
  69.7 0.1 copy.50
  69.7 0.1 select_reduce_fusion
  69.9 0.6 convert_reduce_fusion
  70.5 0.1 copy.53
  70.6 0.7 reshape.128.codes
  71.3 48.5 %shard_map.92 = bf16[2,96,128,128]{3,2,1,0:T(8,128)(2,1)} custom-call(s32[768]{0:T(1024)} %reshape.128.codes, s32[96]{0:T(128)} %get-tuple-element.9.counts, f32[288]{0:T(512)} %reshape.129.dirs, f32[96,128]{1,0:T(8,128)} %reshape.131.toward, f32[32,8,128]{2,1,0:T(8,128)} %reshape.135.geometry, bf16[8,2080,256]{2,1,0:T(8,128)(2,1)} %copy-done.1), custom_call_target="tpu_custom_call" | custom-call | tf_op jit(solution)/shard_map/pallas_call | solution.py:293
  119.8 0.0 copy-start
  119.8 2.8 %copy-done = bf16[2,96,128,128]{3,2,1,0:T(8,128)(2,1)S(1)} copy-done((bf16[2,96,128,128]{3,2,1,0:T(8,128)(2,1)S(1)}, bf16[2,96,128,128]{3,2,1,0:T(8,128)(2,1)}, u32[]{:S(2)}) %copy-start) | copy-done | bytes 6291480
  122.6 39.2 %shard_map.93 = f32[768,256]{1,0:T(8,128)S(1)} custom-call(bf16[2,4,4,6,128,128]{5,4,3,2,1,0:T(8,128)(2,1)S(1)} %bitcast.32), custom_call_target="tpu_custom_call" | custom-call | tf_op jit(solution)/shard_map/pallas_call | solution.py:428
  161.9 0.9 copy.68
  (23 shorter events, 0.3 us)
Async XLA Ops:
  6.4 0.7 copy-start.2
  7.1 0.7 copy-start.3
  7.8 0.7 copy-start.4
  62.1 3.3 %copy-start.1 = (bf16[8,2080,256]{2,1,0:T(8,128)(2,1)}, bf16[8,2080,256]{2,1,0:T(8,128)(2,1)S(1)}, u32[]{:S(2)}) copy-start(bf16[8,2080,256]{2,1,0:T(8,128)(2,1)S(1)} %get-tuple-element.8.signals) | copy-start | bytes 25559044
  119.8 2.8 %copy-start = (bf16[2,96,128,128]{3,2,1,0:T(8,128)(2,1)S(1)}, bf16[2,96,128,128]{3,2,1,0:T(8,128)(2,1)}, u32[]{:S(2)}) copy-start(bf16[2,96,128,128]{3,2,1,0:T(8,128)(2,1)} %shard_map.92) | copy-start | bytes 18874372
